TPU v7x, 32 devices: a whole 2x2x4 slice. The times are simulated.
32 devices in a mesh: row: 2 (over core), col: 16 (over z, y, x).
Axes of the slice: x: 2, y: 2, z: 4, core: 2. Of those that a mesh axis runs over, the one named last changes fastest.
Arguments:
- features: bfloat16 [512, 8192], P('col', 'row'), may hold values from -6 to 6
- a_blocks: bfloat16 [64, 2, 2, 128, 128], P('row'), may hold values from -0.375 to 0.375
- block_cols: int32 [64, 2, 2], P('row'), may hold values from 0 to 31
- block_counts: int32 [64, 2], P('row'), may hold values from 0 to 2
- weight: bfloat16 [512, 512], P('col'), may hold values from -0.25 to 0.25
- cotangent: bfloat16 [512, 8192], P('col', 'row'), may hold values from -6 to 6
Outputs:
- output: bfloat16 [512, 8192], P('col', 'row')
- grad_weight: float32 [512, 512], P('col')
- grad_features: bfloat16 [512, 8192], P('col', 'row')
Inputs may be any that keep to these rules, and one draw needn't show every extreme that they name: `block_cols`: block column indices lie within one slab's blocks.
All inputs are finite; a program needn't handle non-finite values.
Results may differ from a plain program's by a relative error of at most 0.0061.
Values may be sent and summed in bfloat16 or wider, within the bound.
A program may use at most 128 MiB of HBM per device.

v0:
```python
import jax
import jax.numpy as jnp
from jax import lax
from jax.sharding import PartitionSpec as P


def from_root(value, axis, source):
    kept = jnp.where(lax.axis_index(axis) == source, value, 0).astype(value.dtype)
    return lax.psum(kept, axis)


def local(features, a_blocks, block_cols, block_counts, weight, cotangent):
    feat_dev = features.shape[0]
    slab_rows = features.shape[1]
    block_size = a_blocks.shape[-1]
    local_blocks = a_blocks.shape[0]
    section_count = a_blocks.shape[1]
    slot_count = a_blocks.shape[2]
    row_blocks = slab_rows // block_size
    slot_ids = jnp.arange(slot_count, dtype=jnp.int32)
    live_mask = (slot_ids[None, None, :] < block_counts[:, :, None]).astype(jnp.bfloat16)
    masked = a_blocks * live_mask[:, :, :, None, None]
    global_index = (
        jnp.arange(section_count, dtype=jnp.int32)[None, :, None] * row_blocks + block_cols
    )
    node_total = slab_rows * lax.axis_size("row")
    total = jnp.zeros((feat_dev, local_blocks, block_size), jnp.float32)
    for section_idx in range(lax.axis_size("row")):
        panel_rows = from_root(features, "row", section_idx).reshape(
            feat_dev, row_blocks, block_size
        )
        picked = panel_rows[:, block_cols[:, section_idx, :]]
        total = total + jnp.einsum(
            "fbkj,bkij->fbi", picked, masked[:, section_idx], preferred_element_type=jnp.float32
        )
    aggregated = total.reshape(feat_dev, slab_rows).astype(jnp.bfloat16)
    agg_full = lax.all_gather(aggregated, "col", axis=0, tiled=True)
    preact = jnp.dot(weight, agg_full, preferred_element_type=jnp.float32)
    output = jax.nn.silu(preact).astype(jnp.bfloat16)
    sigmoid_pre = jax.nn.sigmoid(preact)
    dpre = (
        cotangent.astype(jnp.float32) * sigmoid_pre * (1.0 + preact * (1.0 - sigmoid_pre))
    ).astype(jnp.bfloat16)
    local_grad = lax.dot_general(
        dpre, agg_full, (((1,), (1,)), ((), ())), preferred_element_type=jnp.float32
    )
    grad_weight = lax.psum(local_grad, "row") / jnp.sqrt(jnp.float32(node_total))
    dpre_full, weight_full = (
        lax.all_gather(dpre, "col", axis=0, tiled=True),
        lax.all_gather(weight, "col", axis=0, tiled=True),
    )
    first_col = lax.axis_index("col") * feat_dev
    weight_cols = lax.dynamic_slice_in_dim(weight_full, first_col, feat_dev, 1)
    dagg = lax.dot_general(
        weight_cols, dpre_full, (((0,), (0,)), ((), ())), preferred_element_type=jnp.float32
    ).astype(jnp.bfloat16)
    contrib = jnp.einsum(
        "fbi,bskij->fbskj",
        dagg.reshape(feat_dev, local_blocks, block_size),
        masked,
        preferred_element_type=jnp.float32,
    )
    terms = (
        jnp.zeros((feat_dev, section_count * row_blocks, block_size), jnp.float32)
        .at[:, global_index]
        .add(contrib)
    )
    terms = terms.reshape(feat_dev, section_count * slab_rows)
    grad_features = lax.psum_scatter(terms, "row", scatter_dimension=1, tiled=True).astype(
        jnp.bfloat16
    )
    return (output, grad_weight, grad_features)


def solution(mesh):
    placed = (
        P("col", "row"),
        P("row", None, None, None, None),
        P("row", None, None),
        P("row", None),
        P("col", None),
        P("col", "row"),
    )
    return jax.shard_map(
        local,
        mesh=mesh,
        in_specs=placed,
        out_specs=(P("col", "row"), P("col", None), P("col", "row")),
        check_vma=False,
    )
```

profile of v0, /device:TPU:5, one launch (start us, length us, event | category | flops | bytes accessed | tf_op | source)
XLA Modules:
  0.0 237.4 jit_solution(17567014226757834611)
XLA Ops:
  7.2 1.0 select_bitcast_fusion
  8.2 0.9 copy_bitcast_fusion.2
  9.2 0.7 compare_select_fusion.1
  9.9 0.1 copy.27
  10.0 0.1 reshape.92
  10.1 0.8 fusion.12
  10.8 0.1 copy.29
  10.9 0.1 reshape.100
  11.0 4.5 %copy_multiply_fusion = bf16[32,2,2,128,128]{4,3,2,0,1:T(8,128)(2,1)} fusion(bf16[32,2,2,128,128]{4,3,2,1,0:T(8,128)(2,1)} %param.7, bf16[32,2,2]{2,0,1:T(8,128)(2,1)S(1)} %fusion.12), kind=kLoop, calls=%fused_computation.7 | loop fusion | flops 2097152 | bytes 8388864 | tf_op jit(solution)/shard_map/mul | solution.py:22
  15.5 16.2 %all-reduce.6.cloned.1.call-done = (bf16[32,32,128]{2,0,1:T(8,128)(2,1)}, bf16[32,32,128]{2,0,1:T(8,128)(2,1)}) async-done(((bf16[32,32,128]{2,0,1:T(8,128)(2,1)}, bf16[32,32,128]{2,0,1:T(8,128)(2,1)}), (bf16[32,32,128]{2,0,1:T(8,128)(2,1)}, bf16[32,32,128]{2,0,1:T(8,128)(2,1)})) %all-reduce.6.cloned.1.call-update) | async-done | bytes 524304 | tf_op jit(solution)/shard_map/psum | solution.py:9
  31.7 1.6 gather_fusion
  33.4 2.4 %fusion.4 = f32[32,128,32]{1,2,0:T(8,128)S(1)} fusion(bf16[32,32,2,128]{3,0,2,1:T(8,128)(2,1)S(1)} %bitcast.82, bf16[32,2,2,128,128]{4,3,2,0,1:T(8,128)(2,1)} %copy_multiply_fusion), kind=kOutput, calls=%fused_computation.12 | convolution fusion | flops 67108864 | bytes 3145728 | tf_op jit(solution)/shard_map/fbkj,bkij->fbi/dot_general | solution.py:33
  35.8 0.7 gather_fusion.1
  36.5 2.4 %fusion.8 = bf16[32,4,8,128]{3,2,1,0:T(8,128)(2,1)S(1)} fusion(f32[32,128,32]{1,2,0:T(8,128)S(1)} %fusion.4, bf16[32,32,2,128]{3,0,2,1:T(8,128)(2,1)S(1)} %bitcast.81, bf16[32,2,2,128,128]{4,3,2,0,1:T(8,128)(2,1)} %copy_multiply_fusion), kind=kOutput, calls=%fused_computation.16 | convolution fusion | flops 67371008 | bytes 3407872 | tf_op jit(solution)/shard_map/fbkj,bkij->fbi/dot_general | solution.py:33
  38.9 0.8 copy.54
  39.8 75.5 %all-gather.3.cloned.1.call-done = bf16[512,4096]{1,0:T(8,128)(2,1)} async-done(((bf16[32,4096]{1,0:T(8,128)(2,1)}), bf16[512,4096]{1,0:T(8,128)(2,1)}) %all-gather.3.cloned.1.call-update) | async-done | bytes 4194320 | tf_op jit(solution)/shard_map/all_gather | solution.py:37
  115.2 3.9 %multiply_convert_fusion = (bf16[32,4096]{1,0:T(8,128)(2,1)}, bf16[32,4096]{1,0:T(8,128)(2,1)}) fusion(bf16[32,4096]{1,0:T(8,128)(2,1)S(1)} %copy-done.4, bf16[32,512]{1,0:T(8,128)(2,1)S(1)} %copy-done.2, bf16[512,4096]{1,0:T(8,128)(2,1)} %all-gather.3.cloned.1.call-done), kind=kOutput, calls=%fused_computation.19 | convolution fusion | flops 135790592 | bytes 5013504 | tf_op jit(solution)/shard_map/dot_general | solution.py:38
  119.3 0.1 copy.31
  119.4 0.1 reshape.108
  119.5 34.8 %all_gather.10 = bf16[512,512]{1,0:T(8,128)(2,1)S(1)} all-gather(bf16[32,512]{1,0:T(8,128)(2,1)S(1)} %copy-done.2), channel_id=1, replica_groups=mesh['row'=2,'col'=16] {'col'}, dimensions={0}, use_global_device_ids=true | all-gather | bytes 557056 | tf_op jit(solution)/shard_map/all_gather | solution.py:50
  154.4 4.3 %fusion.14 = f32[32,512]{1,0:T(8,128)} fusion(bf16[32,4096]{1,0:T(8,128)(2,1)} %get-tuple-element.5, bf16[512,4096]{1,0:T(8,128)(2,1)} %all-gather.3.cloned.1.call-done), kind=kOutput, calls=%fused_computation.39 | convolution fusion | flops 134217728 | bytes 4521984 | tf_op jit(solution)/shard_map/dot_general | solution.py:44
  158.7 37.4 %all-gather.5.cloned.1.call-done = bf16[512,4096]{1,0:T(8,128)(2,1)} async-done(((bf16[32,4096]{1,0:T(8,128)(2,1)}), bf16[512,4096]{1,0:T(8,128)(2,1)}) %all-gather.5.cloned.1.call-update) | async-done | bytes 4194320 | tf_op jit(solution)/shard_map/all_gather | solution.py:49
  196.1 3.3 %fusion.9 = bf16[4,8,32,128]{3,1,2,0:T(8,128)(2,1)S(1)} fusion(bf16[512,4096]{1,0:T(8,128)(2,1)} %all-gather.5.cloned.1.call-done, bf16[512,512]{1,0:T(8,128)(2,1)S(1)} %all_gather.10, s32[]{:T(128)S(6)} %select_n.47), kind=kOutput, calls=%fused_computation.17 | convolution fusion | flops 134348800 | bytes 4587524 | tf_op jit(solution)/shard_map/dot_general | solution.py:54
  199.4 0.1 copy-done
  199.5 0.8 fusion
  200.3 0.1 broadcast_in_dim.18
  200.4 5.7 %scatter_fusion = f32[32,64,128]{2,0,1:T(8,128)S(1)} fusion(f32[32,64,128]{2,0,1:T(8,128)S(1)} %broadcast_in_dim.18, s32[128]{0:T(128)S(1)} %reshape.108, f32[128,32,128]{2,1,0:T(8,128)S(1)} %bitcast.78), kind=kCustom, calls=%fused_computation.2 | custom fusion | flops 524288 | bytes 6291968 | tf_op jit(solution)/shard_map/scatter-add | solution.py:66
  206.2 1.1 copy_bitcast_fusion
  207.3 9.9 %all-reduce.4.cloned.1.call-done = f32[32,512]{1,0:T(8,128)} async-done(((f32[32,512]{1,0:T(8,128)}), f32[32,512]{1,0:T(8,128)}) %all-reduce.4.cloned.1.call-update) | async-done | bytes 65552 | tf_op jit(solution)/shard_map/psum | solution.py:47
  217.2 1.5 broadcast_multiply_fusion
  218.7 10.5 %reduce-scatter.2.cloned.1.call-done = f32[32,4096]{1,0:T(8,128)} async-done(((f32[32,8192]{1,0:T(8,128)}), f32[32,4096]{1,0:T(8,128)}) %reduce-scatter.2.cloned.1.call-update) | async-done | bytes 524304 | tf_op jit(solution)/shard_map/reduce_scatter | solution.py:69
  229.1 1.8 convert_element_type.42
  (24 shorter events, 0.4 us)
Async XLA Ops:
  7.2 24.5 %all-reduce.6.cloned.1.call-start = ((), (), s32[]{:S(2)}) async-start(), calls=%async_computation.5 | async-start | bytes 1048576 | tf_op jit(solution)/shard_map/psum | solution.py:9
  9.1 106.1 %all-gather.3.cloned.1.call-start = ((), (), s32[]{:S(2)}) async-start(), calls=%async_computation.1 | async-start | bytes 4456448 | tf_op jit(solution)/shard_map/all_gather | solution.py:37
  31.7 4.1 %copy-start.1 = (bf16[32,32,128]{2,0,1:T(8,128)(2,1)S(1)}, bf16[32,32,128]{2,0,1:T(8,128)(2,1)}, u32[]{:S(2)}) copy-start(bf16[32,32,128]{2,0,1:T(8,128)(2,1)} %get-tuple-element.4) | copy-start | bytes 786436
  33.4 81.9 %copy-start.2 = (bf16[32,512]{1,0:T(8,128)(2,1)S(1)}, bf16[32,512]{1,0:T(8,128)(2,1)}, u32[]{:S(2)}) copy-start(bf16[32,512]{1,0:T(8,128)(2,1)} %param.10) | copy-start | bytes 98308
  33.4 81.8 %copy-start.4 = (bf16[32,4096]{1,0:T(8,128)(2,1)S(1)}, bf16[32,4096]{1,0:T(8,128)(2,1)}, u32[]{:S(2)}) copy-start(bf16[32,4096]{1,0:T(8,128)(2,1)} %param.11) | copy-start | bytes 786436
  36.5 82.7 %copy-start.3 = (s32[32,2,2]{0,2,1:T(2,128)S(1)}, s32[32,2,2]{0,2,1:T(2,128)}, u32[]{:S(2)}) copy-start(s32[32,2,2]{0,2,1:T(2,128)} %param.8) | copy-start | bytes 1540
  39.7 156.4 %all-gather.5.cloned.1.call-start = ((), (), s32[]{:S(2)}) async-start(), calls=%async_computation.3 | async-start | bytes 4456448 | tf_op jit(solution)/shard_map/all_gather | solution.py:49
  119.1 98.1 %all-reduce.4.cloned.1.call-start = ((), (), s32[]{:S(2)}) async-start(), calls=%async_computation.2 | async-start | bytes 131072 | tf_op jit(solution)/shard_map/psum | solution.py:47
  158.7 70.4 %reduce-scatter.2.cloned.1.call-start = ((), (), s32[]{:S(2)}) async-start(), calls=%async_computation.4 | async-start | bytes 1572864 | tf_op jit(solution)/shard_map/reduce_scatter | solution.py:69
  196.1 3.4 %copy-start = (bf16[32,2,2,128,128]{4,3,2,0,1:T(8,128)(2,1)S(1)}, bf16[32,2,2,128,128]{4,3,2,0,1:T(8,128)(2,1)}, u32[]{:S(2)}) copy-start(bf16[32,2,2,128,128]{4,3,2,0,1:T(8,128)(2,1)} %copy_multiply_fusion) | copy-start | bytes 12582916
Sparse Core Ops, SparseCore 0:
  10.9 20.7 all-reduce.5
  39.8 75.3 all-gather.2
  119.2 76.8 all-gather.4
  198.9 18.2 all-reduce.3
  219.4 9.7 reduce-scatter.1
where the time goes:
time: 239 us; the launch traced here: 237 us
  waiting for transfers between devices  149 us (62%)
  blocking collectives  34.8 us (15%)
  matrix products  17.1 us (7%)
  other arithmetic  16 us (7%)
  between operations  13.9 us (6%)
  local copies, waits for them, and re-layouts  5.95 us (2%)
    all_gather x1, waiting for transfers between devices, local(): agg_full = lax.all_gather(aggregated, 'col', axis=0, tiled=True)  75.5 us
    all_gather x1, waiting for transfers between devices, local(): lax.all_gather(dpre, 'col', axis=0, tiled=True)  37.4 us
    all_gather x1, blocking collectives, local(): lax.all_gather(weight, 'col', axis=0, tiled=True)  34.8 us
    psum x1, waiting for transfers between devices, from_root(): return lax.psum(kept, axis)  16.2 us
    reduce_scatter x1, waiting for transfers between devices, local(): lax.psum_scatter(terms, 'row', scatter_dimension=1, tiled=True)  10.5 us
    psum x1, waiting for transfers between devices, local(): lax.psum(local_grad, 'row') / jnp.sqrt(jnp.float32(node_total))  9.92 us
    scatter-add x1, other arithmetic, local(): terms = jnp.zeros((feat_dev, section_count * row_blocks, block_size), jnp...  5.74 us
    dot_general x2, matrix products, local(): jnp.einsum('fbkj,bkij->fbi', picked, masked[:, section_idx], preferred_el...  4.86 us
  transfers between devices with their start and end apart: 5, of which 5 were waited for; matrix products, arithmetic and copies ran while one was open for 10% of the time, Pallas kernels for 0%

commit v1 on v0

--- a/solution.py
+++ b/solution.py
@@ -1,7 +1,16 @@
+import functools
+import math
+
 import jax
 import jax.numpy as jnp
 from jax import lax
+from jax.experimental import pallas as pl
+from jax.experimental.pallas import tpu as pltpu
 from jax.sharding import PartitionSpec as P
+
+MESH = pl.DeviceIdType.MESH
+f32 = jnp.float32
+bf16 = jnp.bfloat16
 
 
 def from_root(value, axis, source):
@@ -9,7 +18,7 @@
     return lax.psum(kept, axis)
 
 
-def local(features, a_blocks, block_cols, block_counts, weight, cotangent):
+def plain(features, a_blocks, block_cols, block_counts, weight, cotangent):
     feat_dev = features.shape[0]
     slab_rows = features.shape[1]
     block_size = a_blocks.shape[-1]
@@ -72,6 +81,349 @@
     return (output, grad_weight, grad_features)
 
 
+NT = (((1,), (1,)), ((), ()))
+
+
+def link_table(block_cols, block_counts, row_blocks):
+    blocks, sections, slots = block_cols.shape
+    entries = blocks * slots
+    dest = jnp.transpose(block_cols, (1, 0, 2)).reshape(sections, entries)
+    ids = jnp.arange(entries, dtype=jnp.int32)
+    span = jnp.arange(row_blocks, dtype=jnp.int32)
+    keys = jnp.concatenate(
+        [dest, jnp.broadcast_to(span[None], (sections, row_blocks))], axis=1
+    )
+    bound = jnp.concatenate([ids, jnp.full((row_blocks,), entries, jnp.int32)])
+    hit = (dest[:, None, :] == keys[:, :, None]) & (ids[None, None, :] < bound[None, :, None])
+    links = jnp.max(jnp.where(hit, ids[None, None, :] + 1, 0), axis=2)
+    return jnp.concatenate(
+        [block_cols.reshape(-1), block_counts.reshape(-1), links.reshape(-1)]
+    )
+
+
+def kernel(
+    cols_n, scale,
+    meta, feat, a, w, cot,
+    out, gw, gf,
+    av, fv, fb, acc, sagg, aggf, wf, wt, cotf, dpre, sout, sdag, rdag,
+    gpart, grecv, gsend, gin, grow, ghalf, chain, tsend, trecv,
+    loc, cot_s, cot_r, w_s, w_r, wf_s, wf_r, agg_s, agg_r, out_s, out_r,
+    dag_s, dag_r, gw_s, gw_r, pair_s, pair_r,
+):
+    me = lax.axis_index("col")
+    r = lax.axis_index("row")
+    o = 1 - r
+    fd, n = feat.shape
+    nb, sections, slots, bs, _ = a.shape
+    full = wf.shape[0]
+    npd = n // cols_n
+    bpd = npd // bs
+    h = fd // 2
+    entries = nb * slots
+    table = nb * sections * slots
+    links = table + nb * sections
+    per = entries + nb
+    chunk = math.gcd(full, 128)
+
+    def peer(d):
+        return lax.rem(me + d, cols_n)
+
+    def source(d):
+        return lax.rem(me + cols_n - d, cols_n)
+
+    def rows(c, size):
+        return pl.ds(pl.multiple_of(c * size, size), size)
+
+    def remote(src, dst, ss, rs, where):
+        return pltpu.make_async_remote_copy(
+            src_ref=src, dst_ref=dst, send_sem=ss, recv_sem=rs,
+            device_id=where, device_id_type=MESH,
+        )
+
+    def each(fn):
+        @pl.loop(1, cols_n)
+        def _(d):
+            fn(d)
+
+    barrier = pltpu.get_barrier_semaphore()
+    pl.semaphore_signal(barrier, inc=1, device_id={"row": o}, device_id_type=MESH)
+    each(lambda d: pl.semaphore_signal(
+        barrier, inc=1, device_id={"col": peer(d)}, device_id_type=MESH))
+
+    own_feat = pltpu.make_async_copy(feat, fv.at[r], loc.at[0])
+    own_a = pltpu.make_async_copy(a.at[:, r], av.at[:, r], loc.at[1])
+    other_a = pltpu.make_async_copy(a.at[:, o], av.at[:, o], loc.at[2])
+    own_w = pltpu.make_async_copy(w, wf.at[rows(me, fd)], loc.at[3])
+    own_cot = pltpu.make_async_copy(cot.at[:, rows(me, npd)], cotf.at[rows(me, fd)], loc.at[4])
+    own_feat.start()
+    own_a.start()
+    other_a.start()
+    own_w.start()
+    own_cot.start()
+    pl.semaphore_wait(barrier, cols_n)
+
+    swap = remote(feat, fv.at[r], pair_s.at[0], pair_r.at[0], {"row": o})
+    swap_in = remote(feat, fv.at[o], pair_s.at[0], pair_r.at[0], {"row": o})
+    swap.start()
+
+    def half_rows(c, half):
+        return pl.ds(pl.multiple_of(c * fd + half * h, h), h)
+
+    def w_copy(d, c):
+        return remote(w.at[rows(r, h)], wf.at[half_rows(c, r)], w_s.at[d], w_r.at[d],
+                      {"col": peer(d)})
+
+    def cot_copy(d, c):
+        return remote(cot.at[:, rows(peer(d), npd)], cotf.at[rows(c, fd)], cot_s.at[d],
+                      cot_r.at[d], {"col": peer(d)})
+
+    def wf_copy(d, half):
+        part = wf.at[half_rows(source(d), half)]
+        return remote(part, part, wf_s.at[d], wf_r.at[d], {"row": o})
+
+    def agg_copy(d, c):
+        return remote(sagg.at[peer(d)], aggf.at[rows(c, fd)], agg_s.at[d], agg_r.at[d],
+                      {"col": peer(d)})
+
+    def out_copy(d, c):
+        return remote(sout.at[rows(peer(d), fd)], out.at[:, rows(c, npd)], out_s.at[d],
+                      out_r.at[d], {"col": peer(d)})
+
+    def dag_copy(d, c):
+        return remote(sdag.at[rows(peer(d), fd)], rdag.at[:, rows(c, npd)], dag_s.at[d],
+                      dag_r.at[d], {"col": peer(d)})
+
+    def gw_copy(d, c):
+        return remote(gsend.at[peer(d)], gin.at[c], gw_s.at[d], gw_r.at[d],
+                      {"col": peer(d)})
+
+    each(lambda d: w_copy(d, me).start())
+    each(lambda d: cot_copy(d, me).start())
+
+    def alive(count, k):
+        return jnp.minimum(jnp.maximum(count - k, 0), 1).astype(f32)
+
+    def split_blocks(s):
+        for c in range(nb):
+            fb[s, c] = fv[s, :, c * bs:(c + 1) * bs]
+
+    def gathered(b, s):
+        picks = []
+        count = meta[table + b * sections + s]
+        for k in range(slots):
+            c = meta[b * (sections * slots) + s * slots + k]
+            picks.append((fb[s, c].astype(f32) * alive(count, k)).astype(bf16))
+        left = jnp.concatenate(picks, axis=1)
+        right = jnp.concatenate([av[b, s, k] for k in range(slots)], axis=1)
+        return lax.dot_general(left, right, NT, preferred_element_type=f32)
+
+    own_feat.wait()
+    split_blocks(r)
+    own_a.wait()
+
+    @pl.loop(0, nb, unroll=4)
+    def _(b):
+        acc[b] = gathered(b, r)
+
+    swap_in.wait_recv()
+    split_blocks(o)
+    other_a.wait()
+
+    def finish(c):
+        parts = []
+        for j in range(bpd):
+            b = c * bpd + j
+            parts.append((acc[b] + gathered(b, o)).astype(bf16))
+        return jnp.concatenate(parts, axis=1)
+
+    def send_agg(d):
+        sagg[peer(d)] = finish(peer(d))
+        agg_copy(d, me).start()
+
+    each(send_agg)
+    aggf[rows(me, fd), :] = finish(me)
+
+    def forward_w(d):
+        w_copy(d, source(d)).wait_recv()
+        wf_copy(d, r).start()
+
+    each(forward_w)
+    own_w.wait()
+    each(lambda d: wf_copy(d, o).wait_recv())
+    for q in range(full // chunk):
+        wt[:, pl.ds(q * chunk, chunk)] = wf[pl.ds(q * chunk, chunk), :].T
+    own_cot.wait()
+    each(lambda d: cot_copy(d, source(d)).wait_recv())
+    each(lambda d: agg_copy(d, source(d)).wait_recv())
+
+    for q in range(full // chunk):
+        at = pl.ds(q * chunk, chunk)
+        pre = jnp.dot(wf[at, :], aggf[...], preferred_element_type=f32)
+        sig = jax.nn.sigmoid(pre)
+        sout[at, :] = (pre * sig).astype(bf16)
+        dpre[at, :] = (cotf[at, :].astype(f32) * sig * (1.0 + pre * (1.0 - sig))).astype(bf16)
+    for q in range(full // chunk):
+        at = pl.ds(q * chunk, chunk)
+        sdag[at, :] = jnp.dot(wt[at, :], dpre[...], preferred_element_type=f32).astype(bf16)
+
+    each(lambda d: dag_copy(d, me).start())
+    each(lambda d: out_copy(d, me).start())
+    rdag[:, rows(me, npd)] = sdag[rows(me, fd), :]
+    own_out = pltpu.make_async_copy(sout.at[rows(me, fd)], out.at[:, rows(me, npd)], loc.at[5])
+    own_out.start()
+
+    per_chunk = chunk // fd
+    for q in range(full // chunk):
+        part = lax.dot_general(dpre[pl.ds(q * chunk, chunk), :], aggf[...], NT,
+                               preferred_element_type=f32) * scale
+        gpart[pl.ds(q * per_chunk, per_chunk)] = part.reshape(per_chunk, 2, h, full)
+    gswap = remote(gpart.at[:, o], grecv, pair_s.at[1], pair_r.at[1], {"row": o})
+    gswap.start()
+    gswap.wait_recv()
+
+    @pl.loop(0, cols_n)
+    def _(c):
+        gsend[c] = (gpart[c, r] + grecv[c]).astype(bf16)
+
+    gin[me] = gsend[me]
+    each(lambda d: gw_copy(d, me).start())
+
+    each(lambda d: dag_copy(d, source(d)).wait_recv())
+    chain[0] = jnp.zeros(chain.shape[1:], f32)
+
+    def section(s):
+        @pl.loop(0, nb, unroll=2)
+        def _(b):
+            count = meta[table + b * sections + s]
+            right = jnp.concatenate([av[b, s, k] for k in range(slots)], axis=1)
+            terms = jnp.dot(rdag[:, pl.ds(pl.multiple_of(b * bs, bs), bs)], right,
+                            preferred_element_type=f32)
+            for k in range(slots):
+                e = b * slots + k
+                live = alive(count, k)
+                before = chain[meta[links + s * per + e]]
+                chain[e + 1] = before + terms[:, k * bs:(k + 1) * bs] * live
+
+    section(o)
+
+    @pl.loop(0, nb, unroll=4)
+    def _(c):
+        tsend[c] = chain[meta[links + o * per + entries + c]]
+
+    tswap = remote(tsend, trecv, pair_s.at[2], pair_r.at[2], {"row": o})
+    tswap.start()
+    section(r)
+    tswap.wait_recv()
+
+    @pl.loop(0, nb, unroll=4)
+    def _(c):
+        last = chain[meta[links + r * per + entries + c]]
+        gf[:, pl.ds(pl.multiple_of(c * bs, bs), bs)] = (last + trecv[c]).astype(bf16)
+
+    each(lambda d: gw_copy(d, source(d)).wait_recv())
+    total = jnp.zeros((h, full), f32)
+    for c in range(cols_n):
+        total = total + gin[c].astype(f32)
+    ghalf[...] = total
+    gw[rows(r, h), :] = total
+    rswap = remote(ghalf, grow, pair_s.at[3], pair_r.at[3], {"row": o})
+    rswap.start()
+    rswap.wait_recv()
+    gw[rows(o, h), :] = grow[...]
+
+    each(lambda d: out_copy(d, source(d)).wait_recv())
+    own_out.wait()
+
+    def drain(d):
+        w_copy(d, me).wait_send()
+        cot_copy(d, me).wait_send()
+        wf_copy(d, r).wait_send()
+        agg_copy(d, me).wait_send()
+        dag_copy(d, me).wait_send()
+        out_copy(d, me).wait_send()
+        gw_copy(d, me).wait_send()
+
+    each(drain)
+    swap.wait_send()
+    gswap.wait_send()
+    tswap.wait_send()
+    rswap.wait_send()
+
+
+def fused(cols_n, features, a_blocks, block_cols, block_counts, weight, cotangent):
+    fd, n = features.shape
+    nb, sections, slots, bs, _ = a_blocks.shape
+    full = weight.shape[1]
+    npd = n // cols_n
+    h = fd // 2
+    scale = 1.0 / math.sqrt(n * sections)
+    meta = link_table(block_cols, block_counts, n // bs)
+    hbm = pl.BlockSpec(memory_space=pl.ANY)
+    vmem = pl.BlockSpec(memory_space=pltpu.VMEM)
+    dma = pltpu.SemaphoreType.DMA
+    flops = 2 * fd * n * bs * sections * slots * 2 + 6 * full * full * npd
+    return pl.pallas_call(
+        functools.partial(kernel, cols_n, scale),
+        out_shape=(
+            jax.ShapeDtypeStruct((fd, n), bf16),
+            jax.ShapeDtypeStruct((fd, full), f32),
+            jax.ShapeDtypeStruct((fd, n), bf16),
+        ),
+        in_specs=[pl.BlockSpec(memory_space=pltpu.SMEM)] + [hbm] * 4,
+        out_specs=(hbm, vmem, vmem),
+        scratch_shapes=[
+            pltpu.VMEM(a_blocks.shape, bf16),
+            pltpu.VMEM((2, fd, n), bf16),
+            pltpu.VMEM((2, n // bs, fd, bs), bf16),
+            pltpu.VMEM((nb, fd, bs), f32),
+            pltpu.VMEM((cols_n, fd, npd), bf16),
+            pltpu.VMEM((full, npd), bf16),
+            pltpu.VMEM((full, full), bf16),
+            pltpu.VMEM((full, full), bf16),
+            pltpu.VMEM((full, npd), bf16),
+            pltpu.VMEM((full, npd), bf16),
+            pltpu.VMEM((full, npd), bf16),
+            pltpu.VMEM((full, npd), bf16),
+            pltpu.VMEM((fd, n), bf16),
+            pltpu.VMEM((cols_n, 2, h, full), f32),
+            pltpu.VMEM((cols_n, h, full), f32),
+            pltpu.VMEM((cols_n, h, full), bf16),
+            pltpu.VMEM((cols_n, h, full), bf16),
+            pltpu.VMEM((h, full), f32),
+            pltpu.VMEM((h, full), f32),
+            pltpu.VMEM((nb * slots + 1, fd, bs), f32),
+            pltpu.VMEM((nb, fd, bs), f32),
+            pltpu.VMEM((nb, fd, bs), f32),
+            dma((6,)),
+        ] + [dma((cols_n,))] * 14 + [dma((4,))] * 2,
+        compiler_params=pltpu.CompilerParams(
+            collective_id=0, has_side_effects=True, vmem_limit_bytes=40 * 2**20
+        ),
+        cost_estimate=pl.CostEstimate(
+            flops=flops, bytes_accessed=a_blocks.size * 2 + 8 * fd * n,
+            transcendentals=full * npd,
+        ),
+    )(meta, features, a_blocks, weight, cotangent)
+
+
+def local(rows_n, cols_n, features, a_blocks, block_cols, block_counts, weight, cotangent):
+    fd, n = features.shape
+    bs = a_blocks.shape[-1]
+    args = (features, a_blocks, block_cols, block_counts, weight, cotangent)
+    fits = (
+        rows_n == 2
+        and a_blocks.shape[1] == 2
+        and a_blocks.shape[0] * bs == n
+        and bs % 128 == 0
+        and n % (cols_n * bs) == 0
+        and fd % 32 == 0
+        and 128 % fd == 0
+        and weight.shape[1] % 128 == 0
+        and weight.shape[1] == fd * cols_n
+    )
+    return fused(cols_n, *args) if fits else plain(*args)
+
+
 def solution(mesh):
     placed = (
         P("col", "row"),
@@ -82,7 +434,7 @@
         P("col", "row"),
     )
     return jax.shard_map(
-        local,
+        functools.partial(local, mesh.shape["row"], mesh.shape["col"]),
         mesh=mesh,
         in_specs=placed,
         out_specs=(P("col", "row"), P("col", None), P("col", "row")),

time: 239 us -> 58.3 us (0.24)
  the two profiles are of different devices: /device:TPU:5 before, /device:TPU:25 now
where the time goes in v1:
time: 58.3 us; the launch traced here: 58 us
  Pallas kernels  46.7 us (80%)
  local copies, waits for them, and re-layouts  9.64 us (17%)
  other arithmetic  0.94 us (2%)
  between operations  0.67 us (1%)
    pallas_call x1, Pallas kernels, fused(): pl.pallas_call(functools.partial(kernel, cols_n, scale), out_shape=(jax.S...  46.7 us
    unnamed x13, local copies, waits for them, and re-layouts  8.43 us

profile of v1, /device:TPU:25, one launch (start us, length us, event | category | flops | bytes accessed | tf_op | source)
XLA Modules:
  0.0 58.0 jit_solution(3343561533943372733)
XLA Ops:
  0.7 0.7 %iota_compare_fusion = pred[96,64]{0,1:T(8,128)(4,1)S(1)} fusion(s32[96]{0:T(128)} %constant.1.clone.1), kind=kLoop, calls=%fused_computation.1 | loop fusion | flops 6144 | bytes 6528 | tf_op jit(solution)/shard_map/lt | solution.py:97
  1.3 0.8 %copy.16 = s32[32,2]{1,0:T(8,128)S(1)} copy(s32[32,2]{0,1:T(2,128)} %param.9) | data formatting | bytes 512 | tf_op args[3]
  2.1 0.1 reshape.46
  2.2 0.8 %copy.17 = s32[2,32,2]{2,1,0:T(8,128)S(1)} copy(s32[2,32,2]{1,2,0:T(2,128)} %bitcast.1) | data formatting | bytes 1024 | tf_op jit(solution)/shard_map/transpose | solution.py:90
  3.0 0.1 eq.15
  3.1 0.1 pad_add_fusion.1
  3.1 0.1 select_reduce_fusion
  3.3 0.1 reshape.47
  3.3 0.8 %copy.15 = s32[32,2,2]{2,1,0:T(2,128)S(1)} copy(s32[32,2,2]{0,2,1:T(2,128)} %param.8) | data formatting | bytes 1024 | tf_op args[2]
  4.1 0.1 reshape.45
  4.3 0.1 pad_add_fusion.meta
  4.3 0.0 copy-start
  4.3 2.2 %copy-done = bf16[32,2,2,128,128]{4,3,2,1,0:T(8,128)(2,1)S(1)} copy-done((bf16[32,2,2,128,128]{4,3,2,1,0:T(8,128)(2,1)S(1)}, bf16[32,2,2,128,128]{4,3,2,1,0:T(8,128)(2,1)}, u32[]{:S(2)}) %copy-start) | copy-done | bytes 4194328
  6.5 0.0 copy-start.1
  6.5 0.9 %copy-done.1 = bf16[32,4096]{1,0:T(8,128)(2,1)S(1)} copy-done((bf16[32,4096]{1,0:T(8,128)(2,1)S(1)}, bf16[32,4096]{1,0:T(8,128)(2,1)}, u32[]{:S(2)}) %copy-start.1) | copy-done | bytes 262168
  7.5 0.0 copy-start.2
  7.5 0.9 %copy-done.2 = bf16[32,4096]{1,0:T(8,128)(2,1)S(1)} copy-done((bf16[32,4096]{1,0:T(8,128)(2,1)S(1)}, bf16[32,4096]{1,0:T(8,128)(2,1)}, u32[]{:S(2)}) %copy-start.2) | copy-done | bytes 262168
  8.4 0.0 copy-start.3
  8.4 0.8 %copy-done.3 = bf16[32,512]{1,0:T(8,128)(2,1)S(1)} copy-done((bf16[32,512]{1,0:T(8,128)(2,1)S(1)}, bf16[32,512]{1,0:T(8,128)(2,1)}, u32[]{:S(2)}) %copy-start.3) | copy-done | bytes 32792
  9.2 46.7 %shard_map.85 = (bf16[32,4096]{1,0:T(8,128)(2,1)S(1)}, f32[32,512]{1,0:T(8,128)S(1)}, bf16[32,4096]{1,0:T(8,128)(2,1)S(1)}) custom-call(s32[384]{0:T(512)S(1)} %pad_add_fusion.meta, bf16[32,4096]{1,0:T(8,128)(2,1)S(1)} %copy-done.1, bf16[32,2,2,128,128]{4,3,2,1,0:T(8,128)(2,1)S(1)} %copy-done, bf16[32,512]{1,0:T(8,128)(2,1)S(1)} %copy-done.3, ...), custom_call_target="tpu_custom_call" | custom-call | flops 671088640 | bytes 5242880 | tf_op jit(solution)/shard_map/pallas_call | solution.py:365
  55.9 0.7 %copy.21 = bf16[32,4096]{1,0:T(8,128)(2,1)} copy(bf16[32,4096]{1,0:T(8,128)(2,1)S(1)} %get-tuple-element.6) | data formatting | bytes 524288
  56.6 0.6 %copy.22 = f32[32,512]{1,0:T(8,128)} copy(f32[32,512]{1,0:T(8,128)S(1)} %get-tuple-element.7) | data formatting | bytes 131072
  57.3 0.7 %copy.23 = bf16[32,4096]{1,0:T(8,128)(2,1)} copy(bf16[32,4096]{1,0:T(8,128)(2,1)S(1)} %get-tuple-element.8) | data formatting | bytes 524288
  (2 shorter events, 0.0 us)
Async XLA Ops:
  4.3 2.2 %copy-start = (bf16[32,2,2,128,128]{4,3,2,1,0:T(8,128)(2,1)S(1)}, bf16[32,2,2,128,128]{4,3,2,1,0:T(8,128)(2,1)}, u32[]{:S(2)}) copy-start(bf16[32,2,2,128,128]{4,3,2,1,0:T(8,128)(2,1)} %a.1) | copy-start | bytes 12582916
  6.5 0.9 %copy-start.1 = (bf16[32,4096]{1,0:T(8,128)(2,1)S(1)}, bf16[32,4096]{1,0:T(8,128)(2,1)}, u32[]{:S(2)}) copy-start(bf16[32,4096]{1,0:T(8,128)(2,1)} %feat.1) | copy-start | bytes 786436
  7.5 0.9 %copy-start.2 = (bf16[32,4096]{1,0:T(8,128)(2,1)S(1)}, bf16[32,4096]{1,0:T(8,128)(2,1)}, u32[]{:S(2)}) copy-start(bf16[32,4096]{1,0:T(8,128)(2,1)} %cot.1) | copy-start | bytes 786436
  8.4 0.8 %copy-start.3 = (bf16[32,512]{1,0:T(8,128)(2,1)S(1)}, bf16[32,512]{1,0:T(8,128)(2,1)}, u32[]{:S(2)}) copy-start(bf16[32,512]{1,0:T(8,128)(2,1)} %w.1) | copy-start | bytes 98308

commit v2 on v1

--- a/solution.py
+++ b/solution.py
@@ -84,29 +84,27 @@
 NT = (((1,), (1,)), ((), ()))
 
 
-def link_table(block_cols, block_counts, row_blocks):
-    blocks, sections, slots = block_cols.shape
-    entries = blocks * slots
-    dest = jnp.transpose(block_cols, (1, 0, 2)).reshape(sections, entries)
-    ids = jnp.arange(entries, dtype=jnp.int32)
-    span = jnp.arange(row_blocks, dtype=jnp.int32)
-    keys = jnp.concatenate(
-        [dest, jnp.broadcast_to(span[None], (sections, row_blocks))], axis=1
-    )
-    bound = jnp.concatenate([ids, jnp.full((row_blocks,), entries, jnp.int32)])
-    hit = (dest[:, None, :] == keys[:, :, None]) & (ids[None, None, :] < bound[None, :, None])
-    links = jnp.max(jnp.where(hit, ids[None, None, :] + 1, 0), axis=2)
-    return jnp.concatenate(
-        [block_cols.reshape(-1), block_counts.reshape(-1), links.reshape(-1)]
-    )
+def link_rows(block_cols, s, nb, slots):
+    entries = nb * slots
+    lane = lax.broadcasted_iota(jnp.int32, (1, 128), 1)
+    dest = jnp.full((1, 128), -1, jnp.int32)
+    for e in range(entries):
+        dest = jnp.where(lane == e, block_cols[s, e % slots, e // slots], dest)
+    across = jnp.broadcast_to(dest, (128, 128))
+    down = across.T
+    first = lax.broadcasted_iota(jnp.int32, (128, 128), 0)
+    second = lax.broadcasted_iota(jnp.int32, (128, 128), 1)
+    before = jnp.where((down == across) & (first < second), first + 1, 0)
+    last = jnp.where(down == second, first + 1, 0)
+    return jnp.max(before, axis=0, keepdims=True), jnp.max(last, axis=0, keepdims=True)
 
 
 def kernel(
     cols_n, scale,
-    meta, feat, a, w, cot,
+    block_cols, counts, feat, a, w, cot,
     out, gw, gf,
     av, fv, fb, acc, sagg, aggf, wf, wt, cotf, dpre, sout, sdag, rdag,
-    gpart, grecv, gsend, gin, grow, ghalf, chain, tsend, trecv,
+    gpart, grecv, gsend, gin, grow, ghalf, chain, tsend, trecv, table_v, table,
     loc, cot_s, cot_r, w_s, w_r, wf_s, wf_r, agg_s, agg_r, out_s, out_r,
     dag_s, dag_r, gw_s, gw_r, pair_s, pair_r,
 ):
@@ -120,9 +118,6 @@
     bpd = npd // bs
     h = fd // 2
     entries = nb * slots
-    table = nb * sections * slots
-    links = table + nb * sections
-    per = entries + nb
     chunk = math.gcd(full, 128)
 
     def peer(d):
@@ -209,9 +204,9 @@
 
     def gathered(b, s):
         picks = []
-        count = meta[table + b * sections + s]
+        count = counts[s, b]
         for k in range(slots):
-            c = meta[b * (sections * slots) + s * slots + k]
+            c = block_cols[s, k, b]
             picks.append((fb[s, c].astype(f32) * alive(count, k)).astype(bf16))
         left = jnp.concatenate(picks, axis=1)
         right = jnp.concatenate([av[b, s, k] for k in range(slots)], axis=1)
@@ -248,6 +243,12 @@
         wf_copy(d, r).start()
 
     each(forward_w)
+    for s in range(sections):
+        by_entry, by_block = link_rows(block_cols, s, nb, slots)
+        table_v[2 * s:2 * s + 1, :] = by_entry
+        table_v[2 * s + 1:2 * s + 2, :] = by_block
+    put_table = pltpu.make_async_copy(table_v, table, loc.at[6])
+    put_table.start()
     own_w.wait()
     each(lambda d: wf_copy(d, o).wait_recv())
     for q in range(full // chunk):
@@ -288,27 +289,28 @@
     gin[me] = gsend[me]
     each(lambda d: gw_copy(d, me).start())
 
+    put_table.wait()
     each(lambda d: dag_copy(d, source(d)).wait_recv())
     chain[0] = jnp.zeros(chain.shape[1:], f32)
 
     def section(s):
         @pl.loop(0, nb, unroll=2)
         def _(b):
-            count = meta[table + b * sections + s]
+            count = counts[s, b]
             right = jnp.concatenate([av[b, s, k] for k in range(slots)], axis=1)
             terms = jnp.dot(rdag[:, pl.ds(pl.multiple_of(b * bs, bs), bs)], right,
                             preferred_element_type=f32)
             for k in range(slots):
                 e = b * slots + k
                 live = alive(count, k)
-                before = chain[meta[links + s * per + e]]
+                before = chain[table[2 * s, e]]
                 chain[e + 1] = before + terms[:, k * bs:(k + 1) * bs] * live
 
     section(o)
 
     @pl.loop(0, nb, unroll=4)
     def _(c):
-        tsend[c] = chain[meta[links + o * per + entries + c]]
+        tsend[c] = chain[table[2 * o + 1, c]]
 
     tswap = remote(tsend, trecv, pair_s.at[2], pair_r.at[2], {"row": o})
     tswap.start()
@@ -317,7 +319,7 @@
 
     @pl.loop(0, nb, unroll=4)
     def _(c):
-        last = chain[meta[links + r * per + entries + c]]
+        last = chain[table[2 * r + 1, c]]
         gf[:, pl.ds(pl.multiple_of(c * bs, bs), bs)] = (last + trecv[c]).astype(bf16)
 
     each(lambda d: gw_copy(d, source(d)).wait_recv())
@@ -357,7 +359,6 @@
     npd = n // cols_n
     h = fd // 2
     scale = 1.0 / math.sqrt(n * sections)
-    meta = link_table(block_cols, block_counts, n // bs)
     hbm = pl.BlockSpec(memory_space=pl.ANY)
     vmem = pl.BlockSpec(memory_space=pltpu.VMEM)
     dma = pltpu.SemaphoreType.DMA
@@ -369,7 +370,7 @@
             jax.ShapeDtypeStruct((fd, full), f32),
             jax.ShapeDtypeStruct((fd, n), bf16),
         ),
-        in_specs=[pl.BlockSpec(memory_space=pltpu.SMEM)] + [hbm] * 4,
+        in_specs=[pl.BlockSpec(memory_space=pltpu.SMEM)] * 2 + [hbm] * 4,
         out_specs=(hbm, vmem, vmem),
         scratch_shapes=[
             pltpu.VMEM(a_blocks.shape, bf16),
@@ -394,16 +395,18 @@
             pltpu.VMEM((nb * slots + 1, fd, bs), f32),
             pltpu.VMEM((nb, fd, bs), f32),
             pltpu.VMEM((nb, fd, bs), f32),
-            dma((6,)),
+            pltpu.VMEM((8, 128), jnp.int32),
+            pltpu.SMEM((8, 128), jnp.int32),
+            dma((7,)),
         ] + [dma((cols_n,))] * 14 + [dma((4,))] * 2,
         compiler_params=pltpu.CompilerParams(
-            collective_id=0, has_side_effects=True, vmem_limit_bytes=40 * 2**20
+            collective_id=0, has_side_effects=True, vmem_limit_bytes=62 * 2**20
         ),
         cost_estimate=pl.CostEstimate(
             flops=flops, bytes_accessed=a_blocks.size * 2 + 8 * fd * n,
             transcendentals=full * npd,
         ),
-    )(meta, features, a_blocks, weight, cotangent)
+    )(jnp.transpose(block_cols, (1, 2, 0)), block_counts.T, features, a_blocks, weight, cotangent)
 
 
 def local(rows_n, cols_n, features, a_blocks, block_cols, block_counts, weight, cotangent):
@@ -417,6 +420,8 @@
         and bs % 128 == 0
         and n % (cols_n * bs) == 0
         and fd % 32 == 0
+        and a_blocks.shape[0] * a_blocks.shape[2] <= 128
+        and a_blocks.shape[0] <= 128
         and 128 % fd == 0
         and weight.shape[1] % 128 == 0
         and weight.shape[1] == fd * cols_n

time: 58.3 us -> 53.8 us (0.923)
  local copies, waits for them, and re-layouts: 9.64 us -> 4.81 us
  Pallas kernels: 46.7 us -> 48.1 us
  other arithmetic: 0.94 us -> 0 us
    unnamed x13 -> x3, local copies, waits for them, and re-layouts: 8.43 us -> 4.81 us
    pallas_call x1, Pallas kernels: 46.7 us -> 48.1 us  [fused(): pl.pallas_call(functools.partial(kernel, cols_n, scale), out_shape=(jax.S...]
    transpose x1 -> x0, local copies, waits for them, and re-layouts: 0.77 us -> none  [link_table(): dest = jnp.transpose(block_cols, (1, 0, 2)).reshape(sections, entries)]
    lt x1 -> x0, other arithmetic: 0.67 us -> none  [link_table(): ids[None, None, :] < bound[None, :, None]]
where the time goes in v2:
time: 53.8 us; the launch traced here: 53.5 us
  Pallas kernels  48.1 us (89%)
  local copies, waits for them, and re-layouts  4.81 us (9%)
  between operations  0.64 us (1%)
    pallas_call x1, Pallas kernels, fused(): pl.pallas_call(functools.partial(kernel, cols_n, scale), out_shape=(jax.S...  48.1 us
    unnamed x3, local copies, waits for them, and re-layouts  4.81 us

profile of v2, /device:TPU:25, one launch (start us, length us, event | category | flops | bytes accessed | tf_op | source)
XLA Modules:
  0.0 53.5 jit_solution(11357838139056743836)
XLA Ops:
  0.6 48.1 %shard_map.85 = (bf16[32,4096]{1,0:T(8,128)(2,1)}, f32[32,512]{1,0:T(8,128)}, bf16[32,4096]{1,0:T(8,128)(2,1)}) custom-call(s32[2,2,32]{2,1,0:T(2,128)} %bitcast.2, s32[2,32]{1,0:T(2,128)} %bitcast.3, bf16[32,4096]{1,0:T(8,128)(2,1)} %feat.1, bf16[32,2,2,128,128]{4,3,2,1,0:T(8,128)(2,1)} %a.1, bf16[32,512]{1,0:T(8,128)(2,1)} %w.1, bf16[32,4096]{1,0:T(8,128)(2,1)} %cot.1), custom_call_target="tpu_custom_call" | custom-call | flops 671088640 | bytes 5242880 | tf_op jit(solution)/shard_map/pallas_call | solution.py:366
  48.7 1.7 %copy.12 = bf16[32,4096]{1,0:T(8,128)(2,1)} copy(bf16[32,4096]{1,0:T(8,128)(2,1)} %get-tuple-element.6) | data formatting | bytes 524288
  50.4 1.5 %copy.13 = f32[32,512]{1,0:T(8,128)} copy(f32[32,512]{1,0:T(8,128)} %get-tuple-element.7) | data formatting | bytes 131072
  51.9 1.7 %copy.14 = bf16[32,4096]{1,0:T(8,128)(2,1)} copy(bf16[32,4096]{1,0:T(8,128)(2,1)} %get-tuple-element.8) | data formatting | bytes 524288

commit v3 on v2

--- a/solution.py
+++ b/solution.py
@@ -104,9 +104,9 @@
     block_cols, counts, feat, a, w, cot,
     out, gw, gf,
     av, fv, fb, acc, sagg, aggf, wf, wt, cotf, dpre, sout, sdag, rdag,
-    gpart, grecv, gsend, gin, grow, ghalf, chain, tsend, trecv, table_v, table,
+    gpart, grecv, gsend, gnear, gsum, gmid, gfar, grow, ghalf, chain, tsend, trecv, table_v, table,
     loc, cot_s, cot_r, w_s, w_r, wf_s, wf_r, agg_s, agg_r, out_s, out_r,
-    dag_s, dag_r, gw_s, gw_r, pair_s, pair_r,
+    dag_s, dag_r, gw_s, gw_r, gn_s, gn_r, wn_s, wn_r, pair_s, pair_r,
 ):
     me = lax.axis_index("col")
     r = lax.axis_index("row")
@@ -164,16 +164,34 @@
     def half_rows(c, half):
         return pl.ds(pl.multiple_of(c * fd + half * h, h), h)
 
-    def w_copy(d, c):
-        return remote(w.at[rows(r, h)], wf.at[half_rows(c, r)], w_s.at[d], w_r.at[d],
-                      {"col": peer(d)})
+    lo = math.gcd(cols_n, 4)
+    hi = cols_n // lo
+    my_lo = lax.rem(me, lo)
+    my_hi = me // lo
+
+    def near(v):
+        return my_hi * lo + lax.rem(my_lo + v, lo)
+
+    def far(u):
+        return lax.rem(my_hi + u, hi) * lo + my_lo
+
+    def origin(u, v):
+        return lax.rem(my_hi + hi - u, hi) * lo + lax.rem(my_lo + lo - v, lo)
+
+    def w_far(u, c):
+        return remote(w.at[rows(r, h)], wf.at[half_rows(c, r)], w_s.at[u], w_r.at[u],
+                      {"col": far(u)})
+
+    def w_near(u, v, c):
+        part = wf.at[half_rows(c, r)]
+        return remote(part, part, wn_s.at[u, v], wn_r.at[u, v], {"col": near(v)})
 
     def cot_copy(d, c):
         return remote(cot.at[:, rows(peer(d), npd)], cotf.at[rows(c, fd)], cot_s.at[d],
                       cot_r.at[d], {"col": peer(d)})
 
     def wf_copy(d, half):
-        part = wf.at[half_rows(source(d), half)]
+        part = wf.at[half_rows(origin(d // lo, lax.rem(d, lo)), half)]
         return remote(part, part, wf_s.at[d], wf_r.at[d], {"row": o})
 
     def agg_copy(d, c):
@@ -188,11 +206,19 @@
         return remote(sdag.at[rows(peer(d), fd)], rdag.at[:, rows(c, npd)], dag_s.at[d],
                       dag_r.at[d], {"col": peer(d)})
 
-    def gw_copy(d, c):
-        return remote(gsend.at[peer(d)], gin.at[c], gw_s.at[d], gw_r.at[d],
-                      {"col": peer(d)})
-
-    each(lambda d: w_copy(d, me).start())
+    def gw_near(v):
+        return remote(gsend.at[:, lax.rem(my_lo + v, lo)], gnear.at[v], gn_s.at[v], gn_r.at[v],
+                      {"col": near(v)})
+
+    def gw_far(u):
+        return remote(gmid.at[lax.rem(my_hi + u, hi)], gfar.at[u], gw_s.at[u], gw_r.at[u],
+                      {"col": far(u)})
+
+    for u in range(1, hi):
+        w_far(u, me).start()
+    own_w.wait()
+    for v in range(1, lo):
+        w_near(0, v, me).start()
     each(lambda d: cot_copy(d, me).start())
 
     def alive(count, k):
@@ -220,6 +246,11 @@
     def _(b):
         acc[b] = gathered(b, r)
 
+    for u in range(1, hi):
+        w_far(u, origin(u, 0)).wait_recv()
+        for v in range(1, lo):
+            w_near(u, v, origin(u, 0)).start()
+
     swap_in.wait_recv()
     split_blocks(o)
     other_a.wait()
@@ -238,18 +269,17 @@
     each(send_agg)
     aggf[rows(me, fd), :] = finish(me)
 
-    def forward_w(d):
-        w_copy(d, source(d)).wait_recv()
+    for d in range(1, cols_n):
+        u, v = d // lo, d % lo
+        if v:
+            w_near(u, v, origin(u, v)).wait_recv()
         wf_copy(d, r).start()
-
-    each(forward_w)
     for s in range(sections):
         by_entry, by_block = link_rows(block_cols, s, nb, slots)
         table_v[2 * s:2 * s + 1, :] = by_entry
         table_v[2 * s + 1:2 * s + 2, :] = by_block
     put_table = pltpu.make_async_copy(table_v, table, loc.at[6])
     put_table.start()
-    own_w.wait()
     each(lambda d: wf_copy(d, o).wait_recv())
     for q in range(full // chunk):
         wt[:, pl.ds(q * chunk, chunk)] = wf[pl.ds(q * chunk, chunk), :].T
@@ -268,7 +298,6 @@
         sdag[at, :] = jnp.dot(wt[at, :], dpre[...], preferred_element_type=f32).astype(bf16)
 
     each(lambda d: dag_copy(d, me).start())
-    each(lambda d: out_copy(d, me).start())
     rdag[:, rows(me, npd)] = sdag[rows(me, fd), :]
     own_out = pltpu.make_async_copy(sout.at[rows(me, fd)], out.at[:, rows(me, npd)], loc.at[5])
     own_out.start()
@@ -284,10 +313,13 @@
 
     @pl.loop(0, cols_n)
     def _(c):
-        gsend[c] = (gpart[c, r] + grecv[c]).astype(bf16)
-
-    gin[me] = gsend[me]
-    each(lambda d: gw_copy(d, me).start())
+        both = gpart[c, r] + grecv[c]
+        grecv[c] = both
+        gsend[c // lo, lax.rem(c, lo)] = both.astype(bf16)
+
+    for v in range(1, lo):
+        gw_near(v).start()
+    each(lambda d: out_copy(d, me).start())
 
     put_table.wait()
     each(lambda d: dag_copy(d, source(d)).wait_recv())
@@ -314,6 +346,16 @@
 
     tswap = remote(tsend, trecv, pair_s.at[2], pair_r.at[2], {"row": o})
     tswap.start()
+    for v in range(1, lo):
+        gw_near(v).wait_recv()
+    for u in range(hi):
+        level = grecv[u * lo + my_lo]
+        for v in range(1, lo):
+            level = level + gnear[v, u].astype(f32)
+        gsum[u] = level
+        gmid[u] = level.astype(bf16)
+    for u in range(1, hi):
+        gw_far(u).start()
     section(r)
     tswap.wait_recv()
 
@@ -322,10 +364,10 @@
         last = chain[table[2 * r + 1, c]]
         gf[:, pl.ds(pl.multiple_of(c * bs, bs), bs)] = (last + trecv[c]).astype(bf16)
 
-    each(lambda d: gw_copy(d, source(d)).wait_recv())
-    total = jnp.zeros((h, full), f32)
-    for c in range(cols_n):
-        total = total + gin[c].astype(f32)
+    total = gsum[my_hi]
+    for u in range(1, hi):
+        gw_far(u).wait_recv()
+        total = total + gfar[u].astype(f32)
     ghalf[...] = total
     gw[rows(r, h), :] = total
     rswap = remote(ghalf, grow, pair_s.at[3], pair_r.at[3], {"row": o})
@@ -337,15 +379,21 @@
     own_out.wait()
 
     def drain(d):
-        w_copy(d, me).wait_send()
         cot_copy(d, me).wait_send()
         wf_copy(d, r).wait_send()
         agg_copy(d, me).wait_send()
         dag_copy(d, me).wait_send()
         out_copy(d, me).wait_send()
-        gw_copy(d, me).wait_send()
 
     each(drain)
+    for u in range(hi):
+        for v in range(1, lo):
+            w_near(u, v, origin(u, 0)).wait_send()
+    for u in range(1, hi):
+        w_far(u, me).wait_send()
+        gw_far(u).wait_send()
+    for v in range(1, lo):
+        gw_near(v).wait_send()
     swap.wait_send()
     gswap.wait_send()
     tswap.wait_send()
@@ -358,12 +406,14 @@
     full = weight.shape[1]
     npd = n // cols_n
     h = fd // 2
+    lo = math.gcd(cols_n, 4)
+    hi = cols_n // lo
     scale = 1.0 / math.sqrt(n * sections)
     hbm = pl.BlockSpec(memory_space=pl.ANY)
     vmem = pl.BlockSpec(memory_space=pltpu.VMEM)
     dma = pltpu.SemaphoreType.DMA
     flops = 2 * fd * n * bs * sections * slots * 2 + 6 * full * full * npd
-    return pl.pallas_call(
+    results = pl.pallas_call(
         functools.partial(kernel, cols_n, scale),
         out_shape=(
             jax.ShapeDtypeStruct((fd, n), bf16),
@@ -388,8 +438,11 @@
             pltpu.VMEM((fd, n), bf16),
             pltpu.VMEM((cols_n, 2, h, full), f32),
             pltpu.VMEM((cols_n, h, full), f32),
-            pltpu.VMEM((cols_n, h, full), bf16),
-            pltpu.VMEM((cols_n, h, full), bf16),
+            pltpu.VMEM((hi, lo, h, full), bf16),
+            pltpu.VMEM((lo, hi, h, full), bf16),
+            pltpu.VMEM((hi, h, full), f32),
+            pltpu.VMEM((hi, h, full), bf16),
+            pltpu.VMEM((hi, h, full), bf16),
             pltpu.VMEM((h, full), f32),
             pltpu.VMEM((h, full), f32),
             pltpu.VMEM((nb * slots + 1, fd, bs), f32),
@@ -398,7 +451,7 @@
             pltpu.VMEM((8, 128), jnp.int32),
             pltpu.SMEM((8, 128), jnp.int32),
             dma((7,)),
-        ] + [dma((cols_n,))] * 14 + [dma((4,))] * 2,
+        ] + [dma((cols_n,))] * 14 + [dma((lo,))] * 2 + [dma((hi, lo))] * 2 + [dma((4,))] * 2,
         compiler_params=pltpu.CompilerParams(
             collective_id=0, has_side_effects=True, vmem_limit_bytes=62 * 2**20
         ),
@@ -407,6 +460,33 @@
             transcendentals=full * npd,
         ),
     )(jnp.transpose(block_cols, (1, 2, 0)), block_counts.T, features, a_blocks, weight, cotangent)
+    return pl.pallas_call(
+        place,
+        out_shape=tuple(jax.ShapeDtypeStruct(x.shape, x.dtype) for x in results),
+        in_specs=[hbm] * 3,
+        out_specs=(hbm,) * 3,
+        scratch_shapes=[dma((3, 2))],
+        compiler_params=pltpu.CompilerParams(vmem_limit_bytes=62 * 2**20),
+        cost_estimate=pl.CostEstimate(
+            flops=0, bytes_accessed=8 * fd * n + 8 * fd * full, transcendentals=0
+        ),
+    )(*results)
+
+
+def place(*refs):
+    sems = refs[6]
+    copies = []
+    for i in range(3):
+        half = refs[i].shape[0] // 2
+        for j in range(2):
+            at = pl.ds(j * half, half)
+            copies.append(
+                pltpu.make_async_copy(refs[i].at[at], refs[i + 3].at[at], sems.at[i, j])
+            )
+    for copy in copies:
+        copy.start()
+    for copy in copies:
+        copy.wait()
 
 
 def local(rows_n, cols_n, features, a_blocks, block_cols, block_counts, weight, cotangent):

time: 53.8 us -> 62.7 us (1.17)
  the two profiles are of different devices: /device:TPU:25 before, /device:TPU:5 now
where the time goes in v3:
time: 62.7 us; the launch traced here: 62.5 us
  Pallas kernels  61.9 us (99%)
  between operations  0.64 us (1%)
    pallas_call x1, Pallas kernels, fused(): pl.pallas_call(functools.partial(kernel, cols_n, scale), out_shape=(jax.S...  42.8 us
    pallas_call x1, Pallas kernels, fused(): pl.pallas_call(place, out_shape=tuple((jax.ShapeDtypeStruct(x.shape, x.dt...  19 us

profile of v3, /device:TPU:5, one launch (start us, length us, event | category | flops | bytes accessed | tf_op | source)
XLA Modules:
  0.0 62.5 jit_solution(16811171870797765758)
XLA Ops:
  0.6 42.8 %shard_map.85 = (bf16[32,4096]{1,0:T(8,128)(2,1)}, f32[32,512]{1,0:T(8,128)}, bf16[32,4096]{1,0:T(8,128)(2,1)}) custom-call(s32[2,2,32]{2,1,0:T(2,128)} %bitcast.2, s32[2,32]{1,0:T(2,128)} %bitcast.3, bf16[32,4096]{1,0:T(8,128)(2,1)} %feat.1, bf16[32,2,2,128,128]{4,3,2,1,0:T(8,128)(2,1)} %a.1, bf16[32,512]{1,0:T(8,128)(2,1)} %w.1, bf16[32,4096]{1,0:T(8,128)(2,1)} %cot.1), custom_call_target="tpu_custom_call" | custom-call | flops 671088640 | bytes 5242880 | tf_op jit(solution)/shard_map/pallas_call | solution.py:416
  43.5 19.0 %shard_map.86 = (bf16[32,4096]{1,0:T(8,128)(2,1)}, f32[32,512]{1,0:T(8,128)}, bf16[32,4096]{1,0:T(8,128)(2,1)}) custom-call(bf16[32,4096]{1,0:T(8,128)(2,1)} %get-tuple-element.6.refs_0_, f32[32,512]{1,0:T(8,128)} %get-tuple-element.7.refs_1_, bf16[32,4096]{1,0:T(8,128)(2,1)} %get-tuple-element.8.refs_2_), custom_call_target="tpu_custom_call" | custom-call | bytes 1179648 | tf_op jit(solution)/shard_map/pallas_call | solution.py:463

commit v4 on v3

--- a/solution.py
+++ b/solution.py
@@ -84,12 +84,12 @@
 NT = (((1,), (1,)), ((), ()))
 
 
-def link_rows(block_cols, s, nb, slots):
-    entries = nb * slots
+def link_rows(block_cols, s, order, slots):
     lane = lax.broadcasted_iota(jnp.int32, (1, 128), 1)
     dest = jnp.full((1, 128), -1, jnp.int32)
-    for e in range(entries):
-        dest = jnp.where(lane == e, block_cols[s, e % slots, e // slots], dest)
+    for i, b in enumerate(order):
+        for k in range(slots):
+            dest = jnp.where(lane == i * slots + k, block_cols[s, k, b], dest)
     across = jnp.broadcast_to(dest, (128, 128))
     down = across.T
     first = lax.broadcasted_iota(jnp.int32, (128, 128), 0)
@@ -266,7 +266,7 @@
         sagg[peer(d)] = finish(peer(d))
         agg_copy(d, me).start()
 
-    each(send_agg)
+    pl.loop(1, cols_n, unroll=3)(send_agg)
     aggf[rows(me, fd), :] = finish(me)
 
     for d in range(1, cols_n):
@@ -274,8 +274,9 @@
         if v:
             w_near(u, v, origin(u, v)).wait_recv()
         wf_copy(d, r).start()
+    order = [source(d) * bpd + j for d in range(cols_n) for j in range(bpd)]
     for s in range(sections):
-        by_entry, by_block = link_rows(block_cols, s, nb, slots)
+        by_entry, by_block = link_rows(block_cols, s, order, slots)
         table_v[2 * s:2 * s + 1, :] = by_entry
         table_v[2 * s + 1:2 * s + 2, :] = by_block
     put_table = pltpu.make_async_copy(table_v, table, loc.at[6])
@@ -322,23 +323,28 @@
     each(lambda d: out_copy(d, me).start())
 
     put_table.wait()
-    each(lambda d: dag_copy(d, source(d)).wait_recv())
     chain[0] = jnp.zeros(chain.shape[1:], f32)
 
-    def section(s):
-        @pl.loop(0, nb, unroll=2)
-        def _(b):
+    def blocks_of(s, d):
+        for j in range(bpd):
+            i = d * bpd + j
+            b = source(d) * bpd + j
             count = counts[s, b]
             right = jnp.concatenate([av[b, s, k] for k in range(slots)], axis=1)
             terms = jnp.dot(rdag[:, pl.ds(pl.multiple_of(b * bs, bs), bs)], right,
                             preferred_element_type=f32)
             for k in range(slots):
-                e = b * slots + k
-                live = alive(count, k)
+                e = i * slots + k
                 before = chain[table[2 * s, e]]
-                chain[e + 1] = before + terms[:, k * bs:(k + 1) * bs] * live
-
-    section(o)
+                chain[e + 1] = before + terms[:, k * bs:(k + 1) * bs] * alive(count, k)
+
+    blocks_of(o, 0)
+
+    @pl.loop(1, cols_n, unroll=3)
+    def _(d):
+        dag_copy(d, source(d)).wait_recv()
+        blocks_of(o, d)
+
 
     @pl.loop(0, nb, unroll=4)
     def _(c):
@@ -356,7 +362,11 @@
         gmid[u] = level.astype(bf16)
     for u in range(1, hi):
         gw_far(u).start()
-    section(r)
+
+    @pl.loop(0, cols_n, unroll=4)
+    def _(d):
+        blocks_of(r, d)
+
     tswap.wait_recv()
 
     @pl.loop(0, nb, unroll=4)
@@ -465,7 +475,7 @@
         out_shape=tuple(jax.ShapeDtypeStruct(x.shape, x.dtype) for x in results),
         in_specs=[hbm] * 3,
         out_specs=(hbm,) * 3,
-        scratch_shapes=[dma((3, 2))],
+        scratch_shapes=[pltpu.VMEM(x.shape, x.dtype) for x in results] + [dma((3, 2))],
         compiler_params=pltpu.CompilerParams(vmem_limit_bytes=62 * 2**20),
         cost_estimate=pl.CostEstimate(
             flops=0, bytes_accessed=8 * fd * n + 8 * fd * full, transcendentals=0
@@ -474,18 +484,15 @@
 
 
 def place(*refs):
-    sems = refs[6]
-    copies = []
+    sems = refs[9]
+    into = [pltpu.make_async_copy(refs[i], refs[i + 6], sems.at[i, 0]) for i in range(3)]
+    back = [pltpu.make_async_copy(refs[i + 6], refs[i + 3], sems.at[i, 1]) for i in range(3)]
+    for copy in into:
+        copy.start()
     for i in range(3):
-        half = refs[i].shape[0] // 2
-        for j in range(2):
-            at = pl.ds(j * half, half)
-            copies.append(
-                pltpu.make_async_copy(refs[i].at[at], refs[i + 3].at[at], sems.at[i, j])
-            )
-    for copy in copies:
-        copy.start()
-    for copy in copies:
+        into[i].wait()
+        back[i].start()
+    for copy in back:
         copy.wait()
 
 
@@ -504,6 +511,7 @@
         and a_blocks.shape[0] <= 128
         and 128 % fd == 0
         and weight.shape[1] % 128 == 0
+        and cols_n % 4 == 0
         and weight.shape[1] == fd * cols_n
     )
     return fused(cols_n, *args) if fits else plain(*args)

time: 62.7 us -> 44.4 us (0.71)
  Pallas kernels: 61.9 us -> 43.6 us
    pallas_call x1, Pallas kernels: 19 us -> 1.82 us  [fused(): pl.pallas_call(place, out_shape=tuple((jax.ShapeDtypeStruct(x.shape, x.dt...]
    pallas_call x1, Pallas kernels: 42.8 us -> 41.8 us  [fused(): pl.pallas_call(functools.partial(kernel, cols_n, scale), out_shape=(jax.S...]
where the time goes in v4:
time: 44.4 us; the launch traced here: 44.2 us
  Pallas kernels  43.6 us (98%)
  between operations  0.64 us (1%)
    pallas_call x1, Pallas kernels, fused(): pl.pallas_call(functools.partial(kernel, cols_n, scale), out_shape=(jax.S...  41.8 us
    pallas_call x1, Pallas kernels, fused(): pl.pallas_call(place, out_shape=tuple((jax.ShapeDtypeStruct(x.shape, x.dt...  1.82 us

profile of v4, /device:TPU:5, one launch (start us, length us, event | category | flops | bytes accessed | tf_op | source)
XLA Modules:
  0.0 44.2 jit_solution(896753680279662066)
XLA Ops:
  0.6 41.8 %shard_map.85 = (bf16[32,4096]{1,0:T(8,128)(2,1)}, f32[32,512]{1,0:T(8,128)}, bf16[32,4096]{1,0:T(8,128)(2,1)}) custom-call(s32[2,2,32]{2,1,0:T(2,128)} %bitcast.2, s32[2,32]{1,0:T(2,128)} %bitcast.3, bf16[32,4096]{1,0:T(8,128)(2,1)} %feat.1, bf16[32,2,2,128,128]{4,3,2,1,0:T(8,128)(2,1)} %a.1, bf16[32,512]{1,0:T(8,128)(2,1)} %w.1, bf16[32,4096]{1,0:T(8,128)(2,1)} %cot.1), custom_call_target="tpu_custom_call" | custom-call | flops 671088640 | bytes 5242880 | tf_op jit(solution)/shard_map/pallas_call | solution.py:426
  42.4 1.8 %shard_map.86 = (bf16[32,4096]{1,0:T(8,128)(2,1)}, f32[32,512]{1,0:T(8,128)}, bf16[32,4096]{1,0:T(8,128)(2,1)}) custom-call(bf16[32,4096]{1,0:T(8,128)(2,1)} %get-tuple-element.6.refs_0_, f32[32,512]{1,0:T(8,128)} %get-tuple-element.7.refs_1_, bf16[32,4096]{1,0:T(8,128)(2,1)} %get-tuple-element.8.refs_2_), custom_call_target="tpu_custom_call" | custom-call | bytes 1179648 | tf_op jit(solution)/shard_map/pallas_call | solution.py:473

commit v5 on v4

--- a/solution.py
+++ b/solution.py
@@ -194,17 +194,17 @@
         part = wf.at[half_rows(origin(d // lo, lax.rem(d, lo)), half)]
         return remote(part, part, wf_s.at[d], wf_r.at[d], {"row": o})
 
-    def agg_copy(d, c):
-        return remote(sagg.at[peer(d)], aggf.at[rows(c, fd)], agg_s.at[d], agg_r.at[d],
-                      {"col": peer(d)})
-
-    def out_copy(d, c):
-        return remote(sout.at[rows(peer(d), fd)], out.at[:, rows(c, npd)], out_s.at[d],
-                      out_r.at[d], {"col": peer(d)})
-
-    def dag_copy(d, c):
-        return remote(sdag.at[rows(peer(d), fd)], rdag.at[:, rows(c, npd)], dag_s.at[d],
-                      dag_r.at[d], {"col": peer(d)})
+    def agg_copy(j, d, c):
+        return remote(sagg.at[j, peer(d)], aggf.at[j, rows(c, fd)], agg_s.at[j, d],
+                      agg_r.at[j, d], {"col": peer(d)})
+
+    def out_copy(j, d, c):
+        return remote(sout.at[j, rows(peer(d), fd)], out.at[:, rows(c * bpd + j, bs)],
+                      out_s.at[j, d], out_r.at[j, d], {"col": peer(d)})
+
+    def dag_copy(j, d, c):
+        return remote(sdag.at[j, rows(peer(d), fd)], rdag.at[j, c], dag_s.at[j, d],
+                      dag_r.at[j, d], {"col": peer(d)})
 
     def gw_near(v):
         return remote(gsend.at[:, lax.rem(my_lo + v, lo)], gnear.at[v], gn_s.at[v], gn_r.at[v],
@@ -255,26 +255,28 @@
     split_blocks(o)
     other_a.wait()
 
-    def finish(c):
-        parts = []
-        for j in range(bpd):
-            b = c * bpd + j
-            parts.append((acc[b] + gathered(b, o)).astype(bf16))
-        return jnp.concatenate(parts, axis=1)
-
-    def send_agg(d):
-        sagg[peer(d)] = finish(peer(d))
-        agg_copy(d, me).start()
-
-    pl.loop(1, cols_n, unroll=3)(send_agg)
-    aggf[rows(me, fd), :] = finish(me)
-
-    for d in range(1, cols_n):
-        u, v = d // lo, d % lo
-        if v:
-            w_near(u, v, origin(u, v)).wait_recv()
-        wf_copy(d, r).start()
-    order = [source(d) * bpd + j for d in range(cols_n) for j in range(bpd)]
+    def finish(j, c):
+        b = c * bpd + j
+        return (acc[b] + gathered(b, o)).astype(bf16)
+
+    def forward_w():
+        for d in range(1, cols_n):
+            u, v = d // lo, d % lo
+            if v:
+                w_near(u, v, origin(u, v)).wait_recv()
+            wf_copy(d, r).start()
+
+    for j in range(bpd):
+        @pl.loop(1, cols_n, unroll=5)
+        def _(d, j=j):
+            sagg[j, peer(d)] = finish(j, peer(d))
+            agg_copy(j, d, me).start()
+
+        aggf[j, rows(me, fd), :] = finish(j, me)
+        if j == 0:
+            forward_w()
+
+    order = [source(d) * bpd + j for j in range(bpd) for d in range(cols_n)]
     for s in range(sections):
         by_entry, by_block = link_rows(block_cols, s, order, slots)
         table_v[2 * s:2 * s + 1, :] = by_entry
@@ -286,26 +288,35 @@
         wt[:, pl.ds(q * chunk, chunk)] = wf[pl.ds(q * chunk, chunk), :].T
     own_cot.wait()
     each(lambda d: cot_copy(d, source(d)).wait_recv())
-    each(lambda d: agg_copy(d, source(d)).wait_recv())
-
-    for q in range(full // chunk):
-        at = pl.ds(q * chunk, chunk)
-        pre = jnp.dot(wf[at, :], aggf[...], preferred_element_type=f32)
-        sig = jax.nn.sigmoid(pre)
-        sout[at, :] = (pre * sig).astype(bf16)
-        dpre[at, :] = (cotf[at, :].astype(f32) * sig * (1.0 + pre * (1.0 - sig))).astype(bf16)
-    for q in range(full // chunk):
-        at = pl.ds(q * chunk, chunk)
-        sdag[at, :] = jnp.dot(wt[at, :], dpre[...], preferred_element_type=f32).astype(bf16)
-
-    each(lambda d: dag_copy(d, me).start())
-    rdag[:, rows(me, npd)] = sdag[rows(me, fd), :]
-    own_out = pltpu.make_async_copy(sout.at[rows(me, fd)], out.at[:, rows(me, npd)], loc.at[5])
-    own_out.start()
+    own_out = []
+    for j in range(bpd):
+        each(lambda d: agg_copy(j, d, source(d)).wait_recv())
+        span = pl.ds(j * bs, bs)
+        for q in range(full // chunk):
+            at = pl.ds(q * chunk, chunk)
+            pre = jnp.dot(wf[at, :], aggf[j], preferred_element_type=f32)
+            sig = jax.nn.sigmoid(pre)
+            sout[j, at, :] = (pre * sig).astype(bf16)
+            dpre[at, span] = (
+                cotf[at, span].astype(f32) * sig * (1.0 + pre * (1.0 - sig))
+            ).astype(bf16)
+        for q in range(full // chunk):
+            at = pl.ds(q * chunk, chunk)
+            sdag[j, at, :] = jnp.dot(
+                wt[at, :], dpre[:, span], preferred_element_type=f32
+            ).astype(bf16)
+        each(lambda d: dag_copy(j, d, me).start())
+        if j < bpd - 1:
+            each(lambda d: out_copy(j, d, me).start())
+        rdag[j, me] = sdag[j, rows(me, fd), :]
+        own_out.append(pltpu.make_async_copy(
+            sout.at[j, rows(me, fd)], out.at[:, rows(me * bpd + j, bs)], loc.at[7 + j]))
+        own_out[j].start()
 
     per_chunk = chunk // fd
     for q in range(full // chunk):
-        part = lax.dot_general(dpre[pl.ds(q * chunk, chunk), :], aggf[...], NT,
+        right = jnp.concatenate([aggf[j] for j in range(bpd)], axis=1)
+        part = lax.dot_general(dpre[pl.ds(q * chunk, chunk), :], right, NT,
                                preferred_element_type=f32) * scale
         gpart[pl.ds(q * per_chunk, per_chunk)] = part.reshape(per_chunk, 2, h, full)
     gswap = remote(gpart.at[:, o], grecv, pair_s.at[1], pair_r.at[1], {"row": o})
@@ -320,31 +331,29 @@
 
     for v in range(1, lo):
         gw_near(v).start()
-    each(lambda d: out_copy(d, me).start())
+    each(lambda d: out_copy(bpd - 1, d, me).start())
 
     put_table.wait()
     chain[0] = jnp.zeros(chain.shape[1:], f32)
 
-    def blocks_of(s, d):
-        for j in range(bpd):
-            i = d * bpd + j
-            b = source(d) * bpd + j
-            count = counts[s, b]
-            right = jnp.concatenate([av[b, s, k] for k in range(slots)], axis=1)
-            terms = jnp.dot(rdag[:, pl.ds(pl.multiple_of(b * bs, bs), bs)], right,
-                            preferred_element_type=f32)
-            for k in range(slots):
-                e = i * slots + k
-                before = chain[table[2 * s, e]]
-                chain[e + 1] = before + terms[:, k * bs:(k + 1) * bs] * alive(count, k)
-
-    blocks_of(o, 0)
-
-    @pl.loop(1, cols_n, unroll=3)
-    def _(d):
-        dag_copy(d, source(d)).wait_recv()
-        blocks_of(o, d)
-
+    def block_of(s, j, d):
+        i = j * cols_n + d
+        b = source(d) * bpd + j
+        count = counts[s, b]
+        right = jnp.concatenate([av[b, s, k] for k in range(slots)], axis=1)
+        terms = jnp.dot(rdag[j, source(d)], right, preferred_element_type=f32)
+        for k in range(slots):
+            e = i * slots + k
+            before = chain[table[2 * s, e]]
+            chain[e + 1] = before + terms[:, k * bs:(k + 1) * bs] * alive(count, k)
+
+    for j in range(bpd):
+        block_of(o, j, 0)
+
+        @pl.loop(1, cols_n, unroll=5)
+        def _(d, j=j):
+            dag_copy(j, d, source(d)).wait_recv()
+            block_of(o, j, d)
 
     @pl.loop(0, nb, unroll=4)
     def _(c):
@@ -363,9 +372,10 @@
     for u in range(1, hi):
         gw_far(u).start()
 
-    @pl.loop(0, cols_n, unroll=4)
-    def _(d):
-        blocks_of(r, d)
+    for j in range(bpd):
+        @pl.loop(0, cols_n, unroll=4)
+        def _(d, j=j):
+            block_of(r, j, d)
 
     tswap.wait_recv()
 
@@ -385,15 +395,17 @@
     rswap.wait_recv()
     gw[rows(o, h), :] = grow[...]
 
-    each(lambda d: out_copy(d, source(d)).wait_recv())
-    own_out.wait()
+    for j in range(bpd):
+        each(lambda d: out_copy(j, d, source(d)).wait_recv())
+        own_out[j].wait()
 
     def drain(d):
         cot_copy(d, me).wait_send()
         wf_copy(d, r).wait_send()
-        agg_copy(d, me).wait_send()
-        dag_copy(d, me).wait_send()
-        out_copy(d, me).wait_send()
+        for j in range(bpd):
+            agg_copy(j, d, me).wait_send()
+            dag_copy(j, d, me).wait_send()
+            out_copy(j, d, me).wait_send()
 
     each(drain)
     for u in range(hi):
@@ -418,6 +430,7 @@
     h = fd // 2
     lo = math.gcd(cols_n, 4)
     hi = cols_n // lo
+    bpd = npd // bs
     scale = 1.0 / math.sqrt(n * sections)
     hbm = pl.BlockSpec(memory_space=pl.ANY)
     vmem = pl.BlockSpec(memory_space=pltpu.VMEM)
@@ -437,15 +450,15 @@
             pltpu.VMEM((2, fd, n), bf16),
             pltpu.VMEM((2, n // bs, fd, bs), bf16),
             pltpu.VMEM((nb, fd, bs), f32),
-            pltpu.VMEM((cols_n, fd, npd), bf16),
-            pltpu.VMEM((full, npd), bf16),
+            pltpu.VMEM((bpd, cols_n, fd, bs), bf16),
+            pltpu.VMEM((bpd, full, bs), bf16),
             pltpu.VMEM((full, full), bf16),
             pltpu.VMEM((full, full), bf16),
             pltpu.VMEM((full, npd), bf16),
             pltpu.VMEM((full, npd), bf16),
-            pltpu.VMEM((full, npd), bf16),
-            pltpu.VMEM((full, npd), bf16),
-            pltpu.VMEM((fd, n), bf16),
+            pltpu.VMEM((bpd, full, bs), bf16),
+            pltpu.VMEM((bpd, full, bs), bf16),
+            pltpu.VMEM((bpd, cols_n, fd, bs), bf16),
             pltpu.VMEM((cols_n, 2, h, full), f32),
             pltpu.VMEM((cols_n, h, full), f32),
             pltpu.VMEM((hi, lo, h, full), bf16),
@@ -460,8 +473,8 @@
             pltpu.VMEM((nb, fd, bs), f32),
             pltpu.VMEM((8, 128), jnp.int32),
             pltpu.SMEM((8, 128), jnp.int32),
-            dma((7,)),
-        ] + [dma((cols_n,))] * 14 + [dma((lo,))] * 2 + [dma((hi, lo))] * 2 + [dma((4,))] * 2,
+            dma((7 + bpd,)),
+        ] + [dma((cols_n,))] * 6 + [dma((bpd, cols_n))] * 6 + [dma((cols_n,))] * 2 + [dma((lo,))] * 2 + [dma((hi, lo))] * 2 + [dma((4,))] * 2,
         compiler_params=pltpu.CompilerParams(
             collective_id=0, has_side_effects=True, vmem_limit_bytes=62 * 2**20
         ),

time: 44.4 us -> 47.1 us (1.061)
  the two profiles are of different devices: /device:TPU:5 before, /device:TPU:1 now
where the time goes in v5:
time: 47.1 us; the launch traced here: 47 us
  Pallas kernels  46.3 us (98%)
  between operations  0.64 us (1%)
    pallas_call x1, Pallas kernels, fused(): pl.pallas_call(functools.partial(kernel, cols_n, scale), out_shape=(jax.S...  44.5 us
    pallas_call x1, Pallas kernels, fused(): pl.pallas_call(place, out_shape=tuple((jax.ShapeDtypeStruct(x.shape, x.dt...  1.82 us

profile of v5, /device:TPU:1, one launch (start us, length us, event | category | flops | bytes accessed | tf_op | source)
XLA Modules:
  0.0 47.0 jit_solution(6764719910659823363)
XLA Ops:
  0.6 44.5 %shard_map.85 = (bf16[32,4096]{1,0:T(8,128)(2,1)}, f32[32,512]{1,0:T(8,128)}, bf16[32,4096]{1,0:T(8,128)(2,1)}) custom-call(s32[2,2,32]{2,1,0:T(2,128)} %bitcast.2, s32[2,32]{1,0:T(2,128)} %bitcast.3, bf16[32,4096]{1,0:T(8,128)(2,1)} %feat.1, bf16[32,2,2,128,128]{4,3,2,1,0:T(8,128)(2,1)} %a.1, bf16[32,512]{1,0:T(8,128)(2,1)} %w.1, bf16[32,4096]{1,0:T(8,128)(2,1)} %cot.1), custom_call_target="tpu_custom_call" | custom-call | flops 671088640 | bytes 5242880 | tf_op jit(solution)/shard_map/pallas_call | solution.py:439
  45.1 1.8 %shard_map.86 = (bf16[32,4096]{1,0:T(8,128)(2,1)}, f32[32,512]{1,0:T(8,128)}, bf16[32,4096]{1,0:T(8,128)(2,1)}) custom-call(bf16[32,4096]{1,0:T(8,128)(2,1)} %get-tuple-element.6.refs_0_, f32[32,512]{1,0:T(8,128)} %get-tuple-element.7.refs_1_, bf16[32,4096]{1,0:T(8,128)(2,1)} %get-tuple-element.8.refs_2_), custom_call_target="tpu_custom_call" | custom-call | bytes 1179648 | tf_op jit(solution)/shard_map/pallas_call | solution.py:486

commit v6 on v4

--- a/solution.py
+++ b/solution.py
@@ -103,7 +103,7 @@
     cols_n, scale,
     block_cols, counts, feat, a, w, cot,
     out, gw, gf,
-    av, fv, fb, acc, sagg, aggf, wf, wt, cotf, dpre, sout, sdag, rdag,
+    av, fv, fb, acc, sagg, aggf, wh, wf, wt, cotf, dpre, sout, sdag, rdag,
     gpart, grecv, gsend, gnear, gsum, gmid, gfar, grow, ghalf, chain, tsend, trecv, table_v, table,
     loc, cot_s, cot_r, w_s, w_r, wf_s, wf_r, agg_s, agg_r, out_s, out_r,
     dag_s, dag_r, gw_s, gw_r, gn_s, gn_r, wn_s, wn_r, pair_s, pair_r,
@@ -148,7 +148,7 @@
     own_feat = pltpu.make_async_copy(feat, fv.at[r], loc.at[0])
     own_a = pltpu.make_async_copy(a.at[:, r], av.at[:, r], loc.at[1])
     other_a = pltpu.make_async_copy(a.at[:, o], av.at[:, o], loc.at[2])
-    own_w = pltpu.make_async_copy(w, wf.at[rows(me, fd)], loc.at[3])
+    own_w = pltpu.make_async_copy(w.at[rows(r, h)], wh.at[r, me], loc.at[3])
     own_cot = pltpu.make_async_copy(cot.at[:, rows(me, npd)], cotf.at[rows(me, fd)], loc.at[4])
     own_feat.start()
     own_a.start()
@@ -161,9 +161,6 @@
     swap_in = remote(feat, fv.at[o], pair_s.at[0], pair_r.at[0], {"row": o})
     swap.start()
 
-    def half_rows(c, half):
-        return pl.ds(pl.multiple_of(c * fd + half * h, h), h)
-
     lo = math.gcd(cols_n, 4)
     hi = cols_n // lo
     my_lo = lax.rem(me, lo)
@@ -179,31 +176,34 @@
         return lax.rem(my_hi + hi - u, hi) * lo + lax.rem(my_lo + lo - v, lo)
 
     def w_far(u, c):
-        return remote(w.at[rows(r, h)], wf.at[half_rows(c, r)], w_s.at[u], w_r.at[u],
+        return remote(w.at[rows(r, h)], wh.at[r, c], w_s.at[u], w_r.at[u],
                       {"col": far(u)})
 
     def w_near(u, v, c):
-        part = wf.at[half_rows(c, r)]
+        part = wh.at[r, c]
         return remote(part, part, wn_s.at[u, v], wn_r.at[u, v], {"col": near(v)})
 
     def cot_copy(d, c):
-        return remote(cot.at[:, rows(peer(d), npd)], cotf.at[rows(c, fd)], cot_s.at[d],
-                      cot_r.at[d], {"col": peer(d)})
-
-    def wf_copy(d, half):
-        part = wf.at[half_rows(origin(d // lo, lax.rem(d, lo)), half)]
-        return remote(part, part, wf_s.at[d], wf_r.at[d], {"row": o})
+        return remote(cot.at[:, rows(peer(d), npd)], cotf.at[rows(c, fd)], cot_s.at[0],
+                      cot_r.at[0], {"col": peer(d)})
+
+    def bulk(ref, ss, rs):
+        part = ref.at[pl.ds(0, (cols_n - 1) * fd)]
+        return remote(part, part, ss.at[0], rs.at[0], {"row": o})
+
+    def half_copy(half):
+        return remote(wh.at[half], wh.at[half], wf_s.at[0], wf_r.at[0], {"row": o})
 
     def agg_copy(d, c):
-        return remote(sagg.at[peer(d)], aggf.at[rows(c, fd)], agg_s.at[d], agg_r.at[d],
+        return remote(sagg.at[peer(d)], aggf.at[rows(c, fd)], agg_s.at[0], agg_r.at[0],
                       {"col": peer(d)})
 
     def out_copy(d, c):
-        return remote(sout.at[rows(peer(d), fd)], out.at[:, rows(c, npd)], out_s.at[d],
-                      out_r.at[d], {"col": peer(d)})
+        return remote(sout.at[rows(peer(d), fd)], out.at[:, rows(c, npd)], out_s.at[0],
+                      out_r.at[0], {"col": peer(d)})
 
     def dag_copy(d, c):
-        return remote(sdag.at[rows(peer(d), fd)], rdag.at[:, rows(c, npd)], dag_s.at[d],
+        return remote(sdag.at[rows(peer(d), fd)], rdag.at[:, rows(c, npd)], dag_s.at[0],
                       dag_r.at[d], {"col": peer(d)})
 
     def gw_near(v):
@@ -273,7 +273,7 @@
         u, v = d // lo, d % lo
         if v:
             w_near(u, v, origin(u, v)).wait_recv()
-        wf_copy(d, r).start()
+    half_copy(r).start()
     order = [source(d) * bpd + j for d in range(cols_n) for j in range(bpd)]
     for s in range(sections):
         by_entry, by_block = link_rows(block_cols, s, order, slots)
@@ -281,12 +281,15 @@
         table_v[2 * s + 1:2 * s + 2, :] = by_block
     put_table = pltpu.make_async_copy(table_v, table, loc.at[6])
     put_table.start()
-    each(lambda d: wf_copy(d, o).wait_recv())
+    half_copy(o).wait_recv()
+    for c in range(cols_n):
+        for half in range(2):
+            wf[pl.ds(c * fd + half * h, h), :] = wh[half, c]
     for q in range(full // chunk):
         wt[:, pl.ds(q * chunk, chunk)] = wf[pl.ds(q * chunk, chunk), :].T
     own_cot.wait()
-    each(lambda d: cot_copy(d, source(d)).wait_recv())
-    each(lambda d: agg_copy(d, source(d)).wait_recv())
+    bulk(cotf, cot_s, cot_r).wait_recv()
+    bulk(aggf, agg_s, agg_r).wait_recv()
 
     for q in range(full // chunk):
         at = pl.ds(q * chunk, chunk)
@@ -385,17 +388,14 @@
     rswap.wait_recv()
     gw[rows(o, h), :] = grow[...]
 
-    each(lambda d: out_copy(d, source(d)).wait_recv())
+    bulk(sout, out_s, out_r).wait_recv()
     own_out.wait()
 
-    def drain(d):
-        cot_copy(d, me).wait_send()
-        wf_copy(d, r).wait_send()
-        agg_copy(d, me).wait_send()
-        dag_copy(d, me).wait_send()
-        out_copy(d, me).wait_send()
-
-    each(drain)
+    bulk(cotf, cot_s, cot_r).wait_send()
+    bulk(aggf, agg_s, agg_r).wait_send()
+    bulk(sdag, dag_s, dag_r).wait_send()
+    bulk(sout, out_s, out_r).wait_send()
+    half_copy(r).wait_send()
     for u in range(hi):
         for v in range(1, lo):
             w_near(u, v, origin(u, 0)).wait_send()
@@ -439,6 +439,7 @@
             pltpu.VMEM((nb, fd, bs), f32),
             pltpu.VMEM((cols_n, fd, npd), bf16),
             pltpu.VMEM((full, npd), bf16),
+            pltpu.VMEM((2, cols_n, h, full), bf16),
             pltpu.VMEM((full, full), bf16),
             pltpu.VMEM((full, full), bf16),
             pltpu.VMEM((full, npd), bf16),

time: 44.4 us -> 44.2 us (level)
  no operation moved by 1% of the time
where the time goes in v6:
time: 44.2 us; the launch traced here: 44 us
  Pallas kernels  43.3 us (98%)
  between operations  0.64 us (1%)
    pallas_call x1, Pallas kernels, fused(): pl.pallas_call(functools.partial(kernel, cols_n, scale), out_shape=(jax.S...  41.5 us
    pallas_call x1, Pallas kernels, fused(): pl.pallas_call(place, out_shape=tuple((jax.ShapeDtypeStruct(x.shape, x.dt...  1.82 us

profile of v6, /device:TPU:5, one launch (start us, length us, event | category | flops | bytes accessed | tf_op | source)
XLA Modules:
  0.0 44.0 jit_solution(17681084090889502336)
XLA Ops:
  0.6 41.5 %shard_map.85 = (bf16[32,4096]{1,0:T(8,128)(2,1)}, f32[32,512]{1,0:T(8,128)}, bf16[32,4096]{1,0:T(8,128)(2,1)}) custom-call(s32[2,2,32]{2,1,0:T(2,128)} %bitcast.2, s32[2,32]{1,0:T(2,128)} %bitcast.3, bf16[32,4096]{1,0:T(8,128)(2,1)} %feat.1, bf16[32,2,2,128,128]{4,3,2,1,0:T(8,128)(2,1)} %a.1, bf16[32,512]{1,0:T(8,128)(2,1)} %w.1, bf16[32,4096]{1,0:T(8,128)(2,1)} %cot.1), custom_call_target="tpu_custom_call" | custom-call | flops 671088640 | bytes 5242880 | tf_op jit(solution)/shard_map/pallas_call | solution.py:426
  42.2 1.8 %shard_map.86 = (bf16[32,4096]{1,0:T(8,128)(2,1)}, f32[32,512]{1,0:T(8,128)}, bf16[32,4096]{1,0:T(8,128)(2,1)}) custom-call(bf16[32,4096]{1,0:T(8,128)(2,1)} %get-tuple-element.6.refs_0_, f32[32,512]{1,0:T(8,128)} %get-tuple-element.7.refs_1_, bf16[32,4096]{1,0:T(8,128)(2,1)} %get-tuple-element.8.refs_2_), custom_call_target="tpu_custom_call" | custom-call | bytes 1179648 | tf_op jit(solution)/shard_map/pallas_call | solution.py:474

commit v7 on v6

--- a/solution.py
+++ b/solution.py
@@ -302,6 +302,7 @@
         sdag[at, :] = jnp.dot(wt[at, :], dpre[...], preferred_element_type=f32).astype(bf16)
 
     each(lambda d: dag_copy(d, me).start())
+    each(lambda d: out_copy(d, me).start())
     rdag[:, rows(me, npd)] = sdag[rows(me, fd), :]
     own_out = pltpu.make_async_copy(sout.at[rows(me, fd)], out.at[:, rows(me, npd)], loc.at[5])
     own_out.start()
@@ -323,7 +324,6 @@
 
     for v in range(1, lo):
         gw_near(v).start()
-    each(lambda d: out_copy(d, me).start())
 
     put_table.wait()
     chain[0] = jnp.zeros(chain.shape[1:], f32)

time: 44.2 us -> 44.2 us (level)
  no operation moved by 1% of the time
where the time goes in v7:
time: 44.2 us; the launch traced here: 44 us
  Pallas kernels  43.3 us (98%)
  between operations  0.64 us (1%)
    pallas_call x1, Pallas kernels, fused(): pl.pallas_call(functools.partial(kernel, cols_n, scale), out_shape=(jax.S...  41.5 us
    pallas_call x1, Pallas kernels, fused(): pl.pallas_call(place, out_shape=tuple((jax.ShapeDtypeStruct(x.shape, x.dt...  1.82 us

profile of v7, /device:TPU:5, one launch (start us, length us, event | category | flops | bytes accessed | tf_op | source)
XLA Modules:
  0.0 44.0 jit_solution(12685974278945757487)
XLA Ops:
  0.6 41.5 %shard_map.85 = (bf16[32,4096]{1,0:T(8,128)(2,1)}, f32[32,512]{1,0:T(8,128)}, bf16[32,4096]{1,0:T(8,128)(2,1)}) custom-call(s32[2,2,32]{2,1,0:T(2,128)} %bitcast.2, s32[2,32]{1,0:T(2,128)} %bitcast.3, bf16[32,4096]{1,0:T(8,128)(2,1)} %feat.1, bf16[32,2,2,128,128]{4,3,2,1,0:T(8,128)(2,1)} %a.1, bf16[32,512]{1,0:T(8,128)(2,1)} %w.1, bf16[32,4096]{1,0:T(8,128)(2,1)} %cot.1), custom_call_target="tpu_custom_call" | custom-call | flops 671088640 | bytes 5242880 | tf_op jit(solution)/shard_map/pallas_call | solution.py:426
  42.2 1.8 %shard_map.86 = (bf16[32,4096]{1,0:T(8,128)(2,1)}, f32[32,512]{1,0:T(8,128)}, bf16[32,4096]{1,0:T(8,128)(2,1)}) custom-call(bf16[32,4096]{1,0:T(8,128)(2,1)} %get-tuple-element.6.refs_0_, f32[32,512]{1,0:T(8,128)} %get-tuple-element.7.refs_1_, bf16[32,4096]{1,0:T(8,128)(2,1)} %get-tuple-element.8.refs_2_), custom_call_target="tpu_custom_call" | custom-call | bytes 1179648 | tf_op jit(solution)/shard_map/pallas_call | solution.py:474
